TPU v7x, 256 devices: a whole 4x4x8 slice. The times are simulated.
256 devices in a mesh: rows: 64 (over z_hi, x, y, core), cols: 4 (over z_lo).
Axes of the slice: x: 4, y: 4, z: 8 (z_hi: 2, z_lo: 4; z = z_hi * 4 + z_lo), core: 2. Of those that a mesh axis runs over, the one named last changes fastest.
Arguments:
- snapshots: float32 [32768, 4096], P('rows', 'cols'), may hold values from -144 to 144
- partner_slot: int32 [8], replicated, may hold values from 0 to 7, each once
Outputs:
- next_blocks: float32 [32768, 4096], P('rows', 'cols')
- energies: float32 [4096], P('cols')
Inputs may be any that keep to these rules, and one draw needn't show every extreme that they name: `partner_slot`: each of the 8 pair numbers appears exactly once.
All inputs are finite; a program needn't handle non-finite values.
Results may differ from a plain program's by a relative error of at most 0.0001.
Values sent between devices are 32-bit elements; how exact they have to be, the bound alone decides.
A program may use at most 64 MiB of HBM per device.

v0:
```python
import jax
import jax.numpy as jnp
from jax import lax
from jax.sharding import PartitionSpec as P

BW = 256
SWEEPS = 4


def matmul(left, right):
    return jnp.dot(left, right, precision=lax.Precision.HIGHEST, preferred_element_type=jnp.float32)


def inner_products(left, right):
    return jnp.einsum(
        "ri,rj->ij",
        left,
        right,
        precision=lax.Precision.HIGHEST,
        preferred_element_type=jnp.float32,
    )


def damped_rotation(cross_part, diag_left, diag_right):
    half_width = cross_part.shape[0]
    gap_diag = diag_right[None, :] - diag_left[:, None]
    coupling = (
        cross_part
        * gap_diag
        / (
            gap_diag * gap_diag
            + 4.0 * cross_part * cross_part
            + 0.25 * diag_left[:, None] * diag_right[None, :]
        )
    )
    zero_part = jnp.zeros((half_width, half_width), jnp.float32)
    skew = jnp.concatenate(
        [jnp.concatenate([zero_part, coupling], 1), jnp.concatenate([-coupling.T, zero_part], 1)], 0
    )
    norm_scale = 1.0 / jnp.sqrt(1.0 + 2.0 * jnp.sum(coupling * coupling))
    current = (jnp.eye(2 * half_width, dtype=jnp.float32) + skew) * norm_scale
    for sweep in range(SWEEPS):
        product = inner_products(current, current)
        current = 1.5 * current - 0.5 * matmul(current, product)
    return current


def on_device(snapshots, partner_slot):
    rows_here = snapshots.shape[0]
    pairs_here = snapshots.shape[1] // (2 * BW)
    total_rows = rows_here * lax.axis_size("rows")
    lefts = []
    rights = []
    square_parts = []
    for pair_index in range(pairs_here):
        pair_block = snapshots[:, pair_index * 2 * BW : (pair_index + 1) * 2 * BW]
        gram_sum = lax.psum(inner_products(pair_block, pair_block), "rows")
        cross_part = gram_sum[:BW, BW:]
        diagonal = jnp.diagonal(gram_sum)
        rotation = damped_rotation(cross_part, diagonal[:BW], diagonal[BW:])
        rotated = matmul(pair_block, rotation)
        square_parts.append(jnp.sum(rotated * rotated, axis=0))
        lefts.append(rotated[:, :BW])
        rights.append(rotated[:, BW:])
    squares = lax.psum(jnp.concatenate(square_parts), "rows")
    energies = squares / total_rows
    right_stack = jnp.stack(rights)
    first_pair = lax.axis_index("cols") * pairs_here
    own_pairs = first_pair + jnp.arange(pairs_here, dtype=jnp.int32)
    select = (partner_slot[:, None] == own_pairs[None, :]).astype(jnp.float32)
    moved = jnp.einsum(
        "kq,krc->qrc",
        select,
        lax.all_gather(right_stack, "cols", axis=0, tiled=True),
        precision=lax.Precision.HIGHEST,
        preferred_element_type=jnp.float32,
    )
    pieces = []
    for pair_index in range(pairs_here):
        pieces.append(lefts[pair_index])
        pieces.append(moved[pair_index])
    return (jnp.concatenate(pieces, 1), energies)


def solution(mesh):
    in_specs = (P("rows", "cols"), P())
    out_specs = (P("rows", "cols"), P("cols"))
    return jax.shard_map(
        on_device, mesh=mesh, in_specs=in_specs, out_specs=out_specs, check_vma=False
    )
```

profile of v0, /device:TPU:32, one launch (start us, length us, event | category | flops | bytes accessed | tf_op | source)
XLA Modules:
  0.0 1108.9 jit_solution(14846762545368726781)
XLA Ops:
  7.2 4.5 fusion.13
  11.8 2.9 fusion.16
  14.7 790.5 %all-reduce.7.cloned.1.call-done = (f32[512,512]{1,0:T(8,128)}, f32[512,512]{1,0:T(8,128)}) async-done(((f32[512,512]{1,0:T(8,128)}, f32[512,512]{1,0:T(8,128)}), (f32[512,512]{1,0:T(8,128)}, f32[512,512]{1,0:T(8,128)})) %all-reduce.7.cloned.1.call-update) | async-done | bytes 2097168 | tf_op jit(solution)/shard_map/psum | solution.py:57
  805.2 8.6 gather_fusion.1
  813.8 5.0 gather_fusion
  818.8 1.9 multiply_reduce_fusion.2
  821.5 1.1 copy.53
  824.1 1.8 fusion.21
  825.9 1.9 fusion.9
  827.8 1.9 fusion.65
  829.7 1.9 fusion.8
  831.6 1.9 fusion.66
  833.5 2.1 fusion.7
  835.5 1.9 fusion.67
  837.4 1.9 fusion.6
  839.3 1.9 multiply_reduce_fusion.1
  841.3 1.8 fusion.18
  843.1 1.9 fusion.5
  845.0 1.9 fusion.68
  846.9 2.1 fusion.4
  849.0 1.9 fusion.69
  850.8 1.9 fusion.3
  852.7 1.9 fusion.70
  854.6 1.9 fusion.2
  856.5 1.9 multiply_reduce_fusion
  858.4 0.9 fusion.62
  859.3 0.9 fusion.60
  860.3 1.6 copy.38
  861.9 227.3 %psum.23 = f32[1024]{0:T(1024)S(1)} all-reduce(f32[1024]{0:T(1024)S(1)} %pad_maximum_fusion.2), channel_id=1, replica_groups=mesh['rows'=64,'cols'=4] {'rows'}, use_global_device_ids=true, to_apply=%region_6.7 | all-reduce | flops 1024 | bytes 8192 | tf_op jit(solution)/shard_map/psum | solution.py:65
  1089.8 6.4 fusion
  1098.4 1.4 pad_maximum_fusion
  1099.8 1.8 copy.42
  (26 shorter events, 3.9 us)
Async XLA Ops:
  7.2 4.6 copy-start
  7.2 798.0 %all-reduce.7.cloned.1.call-start = ((), (), s32[]{:S(2)}) async-start(), calls=%async_computation.1 | async-start | bytes 4194304 | tf_op jit(solution)/shard_map/psum | solution.py:57
  14.7 1075.1 %all-gather.2.cloned.1.call-start = ((), (), s32[]{:S(2)}) async-start(), calls=%async_computation | async-start | bytes 5242880 | tf_op jit(solution)/shard_map/all_gather | solution.py:74
  805.2 8.6 copy-start.1
  820.8 0.7 copy-start.2
  860.3 229.5 %copy-start.3 = (s32[8]{0:T(128)S(1)}, s32[8]{0:T(128)}, u32[]{:S(2)}) copy-start(s32[8]{0:T(128)} %param.3) | copy-start | bytes 100
Sparse Core Ops, SparseCore 0:
  14.8 790.3 all-reduce.6
  862.0 85.4 all-gather.1
where the time goes:
time: 1110 us
  waiting for transfers between devices  791 us (71%)
  blocking collectives  227 us (20%)
  matrix products  48.1 us (4%)
  local copies, waits for them, and re-layouts  22.8 us (2%)
  between operations  16.1 us (1%)
    psum x1, waiting for transfers between devices, on_device(): gram_sum = lax.psum(inner_products(pair_block, pair_block), 'rows')  790 us
    psum x1, blocking collectives, on_device(): squares = lax.psum(jnp.concatenate(square_parts), 'rows')  227 us
    dot_general x10, matrix products, inner_products(): jnp.einsum('ri,rj->ij', left, right, precision=lax.Precision.HIGHEST, pre...  22.2 us
  transfers between devices with their start and end apart: 2, of which 1 were waited for; matrix products, arithmetic and copies ran while one was open for 0% of the time, Pallas kernels for 0%

commit v1 on v0

v1 whole, which is shorter than its diff:
```python
import functools

import jax
import jax.numpy as jnp
from jax import lax
from jax.experimental import pallas as pl
from jax.experimental.pallas import tpu as pltpu
from jax.sharding import PartitionSpec as P

BW = 256
SWEEPS = 4
MESH = pl.DeviceIdType.MESH
F32 = jnp.float32
BF16 = jnp.bfloat16
XY = 16
CHUNK = 32
LAG = 3


def split(value):
    high = value.astype(BF16)
    return high, (value - high.astype(F32)).astype(BF16)


def dot(left, right, contract=((1,), (0,))):
    return lax.dot_general(left, right, (contract, ((), ())), preferred_element_type=F32)


def dot3(left, right, contract=((1,), (0,))):
    return dot(left[0], right[0], contract) + (
        dot(left[0], right[1], contract) + dot(left[1], right[0], contract)
    )


def coupling_of(cross, diag_tile):
    left_cols = []
    right_rows = []
    for half in range(2):
        left_row = jnp.broadcast_to(diag_tile[half : half + 1, :], (128, 128))
        left_cols.append(jnp.transpose(left_row))
        right_rows.append(diag_tile[2 + half : 3 + half, :])
    left = jnp.concatenate([jnp.concatenate([part, part], 1) for part in left_cols], 0)
    right = jnp.broadcast_to(jnp.concatenate(right_rows, 1), (BW, BW))
    gap = right - left
    return cross * gap / (gap * gap + 4.0 * cross * cross + 0.25 * left * right)


def polynomials(starts, scale):
    eye = (
        lax.broadcasted_iota(jnp.int32, (BW, BW), 0) == lax.broadcasted_iota(jnp.int32, (BW, BW), 1)
    ).astype(F32)
    squares = [(eye + start) * (scale * scale) for start in starts]
    totals = []
    for sweep in range(SWEEPS):
        steps = [1.5 * eye - 0.5 * square for square in squares]
        step_parts = [split(step) for step in steps]
        if sweep == 0:
            totals = [scale * step for step in steps]
        else:
            totals = [dot3(split(total), step) for total, step in zip(totals, step_parts)]
        if sweep < SWEEPS - 1:
            halves = [dot3(split(square), step) for square, step in zip(squares, step_parts)]
            squares = [dot3(split(half), step) for half, step in zip(halves, step_parts)]
    return totals


def pick(options, index):
    value = options[0]
    for position in range(1, len(options)):
        value = jnp.where(index == position, options[position], value)
    return value


def kernel(
    cap, chunks, x_hbm, ps_ref, out_hbm, en_ref,
    own, xh, xl, rh, rl, lefts, rights, fin,
    gmine, gsend, gpeer, rs, zsend, zrecv, ag, rsend, rrecv,
    esend, epeer, exy, ez,
    mid_stage, out_stage, from_outer, from_mid, from_inner,
    load_sem, store_sem, pair_s, pair_r, rs_s, rs_r, z_s, z_r, ag_s, ag_r, ro_s, ro_r,
    e_s, e_r, exy_s, exy_r, in_s, in_r, mid_s, mid_r, out_s, out_r,
):
    row = lax.axis_index("rows")
    z = lax.axis_index("cols")
    core = row % 2
    xy = (row // 2) % XY
    zh = row // (2 * XY)
    side = z // 2
    is_outer = (z % 3) == 0
    is_inner = (z % 3) != 0
    sibling = {"rows": row + 1 - 2 * core}
    far = {"rows": (row + 2 * XY) % (4 * XY)}
    inner_peer = {"cols": 1 + z // 3}
    outer_peer = {"cols": lax.rem(3 * z + 1, 4)}
    mid_peer = {"cols": 3 - z}

    def plane_peer(step):
        return {"rows": zh * 2 * XY + ((xy + step) % XY) * 2 + core}

    def remote(src, dst, send, recv, device):
        return pltpu.make_async_remote_copy(
            src_ref=src, dst_ref=dst, send_sem=send, recv_sem=recv, device_id=device, device_id_type=MESH
        )

    def greet(device):
        pl.semaphore_signal(barrier, inc=1, device_id=device, device_id_type=MESH)

    loads = []
    for pair in range(2):
        load = pltpu.make_async_copy(
            x_hbm.at[:, pl.ds(pair * 2 * BW, 2 * BW)], own.at[pair], load_sem.at[pair]
        )
        load.start()
        loads.append(load)
    barrier = pltpu.get_barrier_semaphore()
    greet(sibling)
    greet(far)

    @pl.loop(1, XY)
    def _(step):
        greet(plane_peer(step))

    @pl.when(is_outer)
    def _():
        greet(inner_peer)

    @pl.when(is_inner)
    def _():
        greet(outer_peer)
        greet(mid_peer)

    for load in loads:
        load.wait()

    def gram(pair, target):
        high, low = split(own[pair])
        xh[pair] = high
        xl[pair] = low
        rows = ((0,), (0,))
        cross = dot3((high[:, :BW], low[:, :BW]), (high[:, BW:], low[:, BW:]), rows)
        target[:, 0:16, :] = cross[:, :128].reshape(XY, 16, 128)
        target[:, 16:32, :] = cross[:, 128:].reshape(XY, 16, 128)
        values = own[pair]
        diagonal = jnp.sum(values * values, axis=0, keepdims=True)
        tile = jnp.concatenate(
            [diagonal[:, 128 * part : 128 * (part + 1)] for part in range(4)]
            + [jnp.zeros((4, 128), F32)],
            0,
        )
        target[:, 32:40, :] = jnp.broadcast_to(tile[None], (XY, 8, 128))

    gram(1 - core, gsend)

    @pl.when(is_outer)
    def _():
        pl.semaphore_wait(barrier, 18)

    @pl.when(is_inner)
    def _():
        pl.semaphore_wait(barrier, 19)

    to_sibling = remote(gsend, gpeer, pair_s, pair_r, sibling)
    to_sibling.start()
    gram(core, gmine)
    to_sibling.wait_recv()
    gmine[...] = gmine[...] + gpeer[...]

    def rs_copy(step):
        target = (xy + step) % XY
        return remote(gmine.at[target], rs.at[xy], rs_s.at[target], rs_r.at[xy], plane_peer(step))

    def rs_arrival(step):
        source = (xy + step) % XY
        return remote(gmine.at[source], rs.at[source], rs_s.at[source], rs_r.at[source], plane_peer(step))

    @pl.loop(1, XY)
    def _(step):
        rs_copy(step).start()

    rs[xy] = gmine[xy]

    @pl.loop(1, XY)
    def _(step):
        rs_arrival(step).wait_recv()

    total = rs[0]
    for chip in range(1, XY):
        total = total + rs[chip]
    zsend[...] = total
    to_far = remote(zsend, zrecv, z_s, z_r, far)
    to_far.start()
    to_far.wait_recv()
    total = zsend[...] + zrecv[...]
    diag_tile = total[32:40, :]
    ag[xy] = total[0:32, :]

    def ag_copy(step):
        return remote(ag.at[xy], ag.at[xy], ag_s.at[step], ag_r.at[xy], plane_peer(step))

    def ag_arrival(step):
        source = (xy + step) % XY
        return remote(ag.at[source], ag.at[source], ag_s.at[step], ag_r.at[source], plane_peer(step))

    @pl.loop(1, XY)
    def _(step):
        ag_copy(step).start()

    @pl.loop(1, XY)
    def _(step):
        ag_arrival(step).wait_recv()

    cross = jnp.concatenate(
        [ag[:, 0:16, :].reshape(BW, 128), ag[:, 16:32, :].reshape(BW, 128)], 1
    )
    coupling = coupling_of(cross, diag_tile)
    scale = lax.rsqrt(jnp.full((1, 1), 1.0, F32) + 2.0 * jnp.sum(coupling * coupling))
    coupling_parts = split(coupling)
    outer_product = dot3(coupling_parts, coupling_parts, ((1,), (1,)))
    inner_product = dot3(coupling_parts, coupling_parts, ((0,), (0,)))
    left_part, right_part = polynomials([outer_product, inner_product], scale)
    rsend[0] = left_part
    rsend[2] = right_part
    rsend[1] = dot3(split(left_part), coupling_parts)
    to_sibling_r = remote(rsend, rrecv, ro_s, ro_r, sibling)
    to_sibling_r.start()

    def spread(pair, source):
        across = source[1]
        for column, row_block, block in (
            (0, 0, source[0]), (1, 0, across), (0, 1, -jnp.transpose(across)), (1, 1, source[2]),
        ):
            high, low = split(block)
            where = (pair, pl.ds(row_block * BW, BW), pl.ds(column * BW, BW))
            rh[where] = high
            rl[where] = low

    rows_here = own.shape[1]
    tile_rows = 128

    def rotate(pair):
        def body(tile, sums):
            rows = pl.ds(pl.multiple_of(tile * tile_rows, tile_rows), tile_rows)
            result = dot3((xh[pair, rows, :], xl[pair, rows, :]), (rh[pair], rl[pair]))
            lefts[pair, rows, :] = result[:, :BW]
            rights[pair, rows, :] = result[:, BW:]
            return sums + jnp.sum(result * result, axis=0, keepdims=True)

        sums = lax.fori_loop(0, rows_here // tile_rows, body, jnp.zeros((1, 2 * BW), F32))
        esend[pair] = jnp.concatenate(
            [sums[:, 128 * part : 128 * (part + 1)] for part in range(4)]
            + [jnp.zeros((4, 128), F32)],
            0,
        )

    spread(core, rsend)
    rotate(core)
    to_sibling_r.wait_recv()
    spread(1 - core, rrecv)
    rotate(1 - core)

    stores = []
    for pair in range(2):
        store = pltpu.make_async_copy(
            lefts.at[pair], out_hbm.at[:, pl.ds(pair * 2 * BW, BW)], store_sem.at[pair]
        )
        store.start()
        stores.append(store)
    e_sibling = remote(esend, epeer, e_s.at[0], e_r.at[0], sibling)
    e_sibling.start()

    slots = []
    for first, second in zip((2, 3, 0, 1, 4, 5, 6, 7), (4, 5, 6, 7, 2, 3, 0, 1)):
        slot = ps_ref[first + side * (second - first)]
        low_side = jnp.where(slot < 2, slot + 2, jnp.where(slot < 4, slot - 2, slot))
        high_side = jnp.where(slot < 2, slot + 6, jnp.where(slot < 4, slot + 2, slot - 4))
        slots.append(jnp.where(side == 0, low_side, high_side))

    def ranks(order, wanted):
        count = jnp.int32(0)
        result = {}
        for position in order:
            result[position] = count
            count = count + jnp.where(wanted(slots[position]), 1, 0)
        return result

    def source_of(order, wanted, rank, entry, default):
        found = default
        for position in order:
            hit = wanted(slots[position]) & (rank[position] == entry) if rank else wanted(slots[position])
            found = jnp.where(hit, order[position], found)
        return found

    crosses = lambda slot: slot >= 4
    returns = lambda slot: slot < 4
    outward = lambda slot: (slot == 2) | (slot == 3)
    zero = jnp.int32(0)
    send_rank = ranks((0, 1, 2, 3), crosses)
    recv_rank = ranks((4, 5, 6, 7), returns)
    out_rank = ranks((0, 1, 4, 5, 6, 7), outward)
    mid_from = [
        source_of({0: 0, 1: 1, 2: 2, 3: 3}, crosses, send_rank, entry, zero) for entry in range(cap)
    ]
    out_places = {0: 0, 1: 1, 4: 2 + recv_rank[4], 5: 2 + recv_rank[5], 6: 2 + recv_rank[6], 7: 2 + recv_rank[7]}
    out_from = [source_of(out_places, outward, out_rank, entry, zero) for entry in range(2)]
    inner_places = {0: 0, 1: 1, 2: 2, 3: 3, 4: 4 + recv_rank[4], 5: 4 + recv_rank[5], 6: 4 + recv_rank[6], 7: 4 + recv_rank[7]}
    outer_places = {2: 0, 3: 1, 0: 2 + out_rank[0], 1: 2 + out_rank[1], 4: 2 + out_rank[4], 5: 2 + out_rank[5], 6: 2 + out_rank[6], 7: 2 + out_rank[7]}
    inner_from = [
        source_of(inner_places, functools.partial(lax.eq, jnp.int32(entry)), None, entry, zero)
        for entry in range(2)
    ]
    outer_from = [
        source_of(outer_places, functools.partial(lax.eq, jnp.int32(2 + entry)), None, entry, zero)
        for entry in range(2)
    ]

    def piece(index):
        return pl.ds(pl.multiple_of(index * CHUNK, CHUNK), CHUNK)

    def in_copy(index):
        return remote(
            rights.at[:, piece(index)], from_outer.at[:, piece(index)],
            in_s.at[index], in_r.at[index], inner_peer,
        )

    def in_arrival(index):
        return remote(
            rights.at[:, piece(index)], from_outer.at[:, piece(index)],
            in_s.at[index], in_r.at[index], outer_peer,
        )

    def mid_copy(index):
        return remote(
            mid_stage.at[:, piece(index)], from_mid.at[:, piece(index)],
            mid_s.at[index], mid_r.at[index], mid_peer,
        )

    def out_copy(index):
        return remote(
            out_stage.at[:, piece(index)], from_inner.at[:, piece(index)],
            out_s.at[index], out_r.at[index], outer_peer,
        )

    def out_arrival(index):
        return remote(
            out_stage.at[:, piece(index)], from_inner.at[:, piece(index)],
            out_s.at[index], out_r.at[index], inner_peer,
        )

    def inner_forward(index):
        in_arrival(index).wait_recv()
        rows = piece(index)
        options = [rights[0, rows, :], rights[1, rows, :], from_outer[0, rows, :], from_outer[1, rows, :]]
        for entry in range(cap):
            mid_stage[entry, rows, :] = pick(options, mid_from[entry])
        mid_copy(index).start()

    def inner_return(index):
        mid_copy(index).wait_recv()
        rows = piece(index)
        near = [rights[0, rows, :], rights[1, rows, :]]
        beyond = [from_mid[entry, rows, :] for entry in range(cap)]
        for entry in range(2):
            out_stage[entry, rows, :] = pick(near + beyond, out_from[entry])
        out_copy(index).start()
        options = near + [from_outer[0, rows, :], from_outer[1, rows, :]] + beyond
        for entry in range(2):
            fin[entry, rows, :] = pick(options, inner_from[entry])

    def outer_finish(index):
        out_arrival(index).wait_recv()
        rows = piece(index)
        options = [rights[0, rows, :], rights[1, rows, :], from_inner[0, rows, :], from_inner[1, rows, :]]
        for entry in range(2):
            fin[entry, rows, :] = pick(options, outer_from[entry])

    @pl.when(is_outer)
    def _():
        @pl.loop(0, chunks)
        def _(index):
            in_copy(index).start()

    @pl.when(is_inner)
    def _():
        @pl.loop(0, LAG)
        def _(index):
            inner_forward(index)

    def advance(first, last):
        @pl.when(is_inner)
        def _():
            @pl.loop(first, last)
            def _(index):
                @pl.when(index < chunks - LAG)
                def _():
                    inner_forward(index + LAG)

                inner_return(index)

        @pl.when(is_outer)
        def _():
            @pl.loop(first, last)
            def _(index):
                outer_finish(index)

    def exy_copy(step):
        return remote(exy.at[xy], exy.at[xy], exy_s.at[step], exy_r.at[xy], plane_peer(step))

    def exy_arrival(step):
        source = (xy + step) % XY
        return remote(exy.at[source], exy.at[source], exy_s.at[step], exy_r.at[source], plane_peer(step))

    first_cut = chunks // 8
    second_cut = chunks // 2 + chunks // 16
    advance(0, first_cut)
    e_sibling.wait_recv()
    exy[xy] = esend[...] + epeer[...]

    @pl.loop(1, XY)
    def _(step):
        exy_copy(step).start()

    advance(first_cut, second_cut)

    @pl.loop(1, XY)
    def _(step):
        exy_arrival(step).wait_recv()

    plane_sum = exy[0]
    for chip in range(1, XY):
        plane_sum = plane_sum + exy[chip]
    ez[0] = plane_sum
    e_far = remote(ez.at[0], ez.at[1], e_s.at[1], e_r.at[1], far)
    e_far.start()
    advance(second_cut, chunks)
    for pair in range(2):
        store = pltpu.make_async_copy(
            fin.at[pair], out_hbm.at[:, pl.ds(pair * 2 * BW + BW, BW)], store_sem.at[2 + pair]
        )
        store.start()
        stores.append(store)
    e_far.wait_recv()
    energies = (ez[0] + ez[1]) / (4 * XY * rows_here)
    en_ref[0:4, :] = energies[0, 0:4, :]
    en_ref[4:8, :] = energies[1, 0:4, :]

    to_sibling.wait_send()
    to_sibling_r.wait_send()
    to_far.wait_send()
    e_sibling.wait_send()
    e_far.wait_send()

    @pl.loop(1, XY)
    def _(step):
        rs_copy(step).wait_send()
        ag_copy(step).wait_send()
        exy_copy(step).wait_send()

    @pl.when(is_outer)
    def _():
        @pl.loop(0, chunks)
        def _(index):
            in_copy(index).wait_send()

    @pl.when(is_inner)
    def _():
        @pl.loop(0, chunks)
        def _(index):
            mid_copy(index).wait_send()
            out_copy(index).wait_send()

    for store in stores:
        store.wait()


def call(cap, snapshots, partner_slot):
    rows = snapshots.shape[0]
    chunks = rows // CHUNK
    block = (rows, BW)
    dma = pltpu.SemaphoreType.DMA
    scratch = [
        pltpu.VMEM((2, rows, 2 * BW), F32),
        pltpu.VMEM((2, rows, 2 * BW), BF16),
        pltpu.VMEM((2, rows, 2 * BW), BF16),
        pltpu.VMEM((2, 2 * BW, 2 * BW), BF16),
        pltpu.VMEM((2, 2 * BW, 2 * BW), BF16),
        pltpu.VMEM((2, *block), F32),
        pltpu.VMEM((2, *block), F32),
        pltpu.VMEM((2, *block), F32),
        pltpu.VMEM((XY, 40, 128), F32),
        pltpu.VMEM((XY, 40, 128), F32),
        pltpu.VMEM((XY, 40, 128), F32),
        pltpu.VMEM((XY, 40, 128), F32),
        pltpu.VMEM((40, 128), F32),
        pltpu.VMEM((40, 128), F32),
        pltpu.VMEM((XY, 32, 128), F32),
        pltpu.VMEM((3, BW, BW), F32),
        pltpu.VMEM((3, BW, BW), F32),
        pltpu.VMEM((2, 8, 128), F32),
        pltpu.VMEM((2, 8, 128), F32),
        pltpu.VMEM((XY, 2, 8, 128), F32),
        pltpu.VMEM((2, 2, 8, 128), F32),
        pltpu.VMEM((cap, *block), F32),
        pltpu.VMEM((2, *block), F32),
        pltpu.VMEM((2, *block), F32),
        pltpu.VMEM((cap, *block), F32),
        pltpu.VMEM((2, *block), F32),
        dma((2,)), dma((4,)), dma, dma, dma((XY,)), dma((XY,)), dma, dma,
        dma((XY,)), dma((XY,)), dma, dma,
        dma((2,)), dma((2,)), dma((XY,)), dma((XY,)),
        dma((chunks,)), dma((chunks,)), dma((chunks,)), dma((chunks,)), dma((chunks,)), dma((chunks,)),
    ]
    return pl.pallas_call(
        functools.partial(kernel, cap, chunks),
        out_shape=(
            jax.ShapeDtypeStruct(snapshots.shape, F32),
            jax.ShapeDtypeStruct((8, 128), F32),
        ),
        in_specs=[pl.BlockSpec(memory_space=pl.ANY), pl.BlockSpec(memory_space=pltpu.SMEM)],
        out_specs=(pl.BlockSpec(memory_space=pl.ANY), pl.BlockSpec(memory_space=pltpu.VMEM)),
        scratch_shapes=scratch,
        name=f"round_{cap}",
        compiler_params=pltpu.CompilerParams(
            collective_id=cap, has_side_effects=True, vmem_limit_bytes=48 << 20
        ),
    )(snapshots, partner_slot)


def on_device(snapshots, partner_slot):
    crossing = jnp.sum((partner_slot[:4] >= 4).astype(jnp.int32))
    moved, energies = lax.cond(
        crossing <= 2,
        functools.partial(call, 2),
        functools.partial(call, 4),
        snapshots,
        partner_slot,
    )
    return moved, energies.reshape(-1)


def solution(mesh):
    in_specs = (P("rows", "cols"), P())
    out_specs = (P("rows", "cols"), P("cols"))
    return jax.shard_map(
        on_device, mesh=mesh, in_specs=in_specs, out_specs=out_specs, check_vma=False
    )
```

time: 1110 us -> 77.2 us (0.07)
  the two profiles are of different devices: /device:TPU:32 before, /device:TPU:1 now
where the time goes in v1:
time: 77.2 us; the launch traced here: 77.1 us
  Pallas kernels  72.6 us (94%)
  local copies, waits for them, and re-layouts  1.91 us (2%)
  other arithmetic  1.29 us (2%)
  between operations  1.29 us (2%)
    pallas_call x1, Pallas kernels, call(): pl.pallas_call(functools.partial(kernel, cap, chunks), out_shape=(jax.Sha...  72.6 us
    unnamed x2, local copies, waits for them, and re-layouts  1.91 us

profile of v1, /device:TPU:1, one launch (start us, length us, event | category | flops | bytes accessed | tf_op | source)
XLA Modules:
  0.0 77.1 jit_solution(17740718452312922905)
XLA Ops:
  0.6 1.3 %fusion = s32[]{:T(128)} fusion(s32[8]{0:T(128)} %param.5), kind=kLoop, calls=%fused_computation.1 | loop fusion | flops 11 | bytes 20 | tf_op jit(solution)/shard_map/reduce_sum | solution.py:529
  2.6 72.6 %conditional.1 = (f32[512,1024]{1,0:T(8,128)S(1)}, f32[1024]{0:T(1024)S(1)}) conditional(s32[]{:T(128)} %convert_element_type.7, (f32[512,1024]{1,0:T(8,128)}, s32[8]{0:T(128)}) %tuple.17, (f32[512,1024]{1,0:T(8,128)}, s32[8]{0:T(128)}) %tuple.17), branch_computations={%region_1.0_spmd, %region_2.0_spmd} | conditional | bytes 16 | solution.py:530
  2.6 72.6 %round_2.1 = (f32[512,1024]{1,0:T(8,128)S(1)}, f32[8,128]{1,0:T(8,128)S(1)}) custom-call(f32[512,1024]{1,0:T(8,128)} %get-tuple-element.27.x_hbm, s32[8]{0:T(128)} %get-tuple-element.18.ps_ref), custom_call_target="tpu_custom_call" | custom-call | tf_op jit(solution)/shard_map/cond/branch_1_fun/round_2/pallas_call | solution.py:512
  75.2 1.3 %copy.14 = f32[512,1024]{1,0:T(8,128)} copy(f32[512,1024]{1,0:T(8,128)S(1)} %get-tuple-element.34) | data formatting | bytes 4194304
  76.5 0.6 copy.15

commit v2 on v0

v2 whole, which is shorter than its diff:
```python
import functools
import types

import jax
import jax.numpy as jnp
from jax import lax
from jax.experimental import pallas as pl
from jax.experimental.pallas import tpu as pltpu
from jax.sharding import PartitionSpec as P

BW = 256
SWEEPS = 4
MESH = pl.DeviceIdType.MESH
F32 = jnp.float32
BF16 = jnp.bfloat16
XY = 16
RAW_CHUNK = 16
LATE_CHUNK = 16
RAW_FIRST = {2: 4, 3: 3, 4: 2}
RAW_ROWS = {2: 192, 3: 128, 4: 96}


def split(value):
    high = value.astype(BF16)
    return high, (value - high.astype(F32)).astype(BF16)


def dot(left, right, contract=((1,), (0,))):
    return lax.dot_general(left, right, (contract, ((), ())), preferred_element_type=F32)


def dot3(left, right, contract=((1,), (0,))):
    return dot(left[0], right[0], contract) + (
        dot(left[0], right[1], contract) + dot(left[1], right[0], contract)
    )


def coupling_of(pieces, diag_tile):
    cross = jnp.concatenate(
        [pieces[:, 0:16, :].reshape(BW, 128), pieces[:, 16:32, :].reshape(BW, 128)], 1
    )
    left_cols = []
    right_rows = []
    for half in range(2):
        left_row = jnp.broadcast_to(diag_tile[half : half + 1, :], (128, 128))
        left_cols.append(jnp.transpose(left_row))
        right_rows.append(diag_tile[2 + half : 3 + half, :])
    left = jnp.concatenate([jnp.concatenate([part, part], 1) for part in left_cols], 0)
    right = jnp.broadcast_to(jnp.concatenate(right_rows, 1), (BW, BW))
    gap = right - left
    coupling = cross * gap / (gap * gap + 4.0 * cross * cross + 0.25 * left * right)
    scale = lax.rsqrt(jnp.full((1, 1), 1.0, F32) + 2.0 * jnp.sum(coupling * coupling))
    return coupling, scale


def polynomials(starts, scale, between):
    eye = (
        lax.broadcasted_iota(jnp.int32, (BW, BW), 0) == lax.broadcasted_iota(jnp.int32, (BW, BW), 1)
    ).astype(F32)
    squares = [(eye + start) * (scale * scale) for start in starts]
    totals = []
    for sweep in range(SWEEPS):
        steps = [1.5 * eye - 0.5 * square for square in squares]
        step_parts = [split(step) for step in steps]
        if sweep == 0:
            totals = [scale * step for step in steps]
            halves = [dot3(split(square), step) for square, step in zip(squares, step_parts)]
        elif sweep == SWEEPS - 1:
            return [dot3(split(total), step) for total, step in zip(totals, step_parts)]
        else:
            stacks = [jnp.concatenate(parts, 0) for parts in zip(totals, squares)]
            stacks = [dot3(split(stack), step) for stack, step in zip(stacks, step_parts)]
            totals = [stack[:BW] for stack in stacks]
            halves = [stack[BW:] for stack in stacks]
        squares = [dot3(split(half), step) for half, step in zip(halves, step_parts)]
        between(sweep)


def pick(options, index):
    value = options[0]
    for position in range(1, len(options)):
        value = jnp.where(index == position, options[position], value)
    return value


def remote(src, dst, send, recv, device):
    return pltpu.make_async_remote_copy(
        src_ref=src, dst_ref=dst, send_sem=send, recv_sem=recv, device_id=device, device_id_type=MESH
    )


def row_of(values):
    return jnp.concatenate(
        [values[:, 128 * part : 128 * (part + 1)] for part in range(4)] + [jnp.zeros((4, 128), F32)], 0
    )


class Stream:
    def __init__(self, whole, near, first, count, chunk, refs, routes, put, fin_first, place):
        self.whole = whole
        self.forwards = self.backs = 0
        self.near, self.first, self.count, self.chunk, self.refs = near, first, count, chunk, refs
        self.routes, self.put, self.fin_first, self.place = routes, put, fin_first, place

    def rows(self, index, offset=0):
        return pl.ds(pl.multiple_of(offset + index * self.chunk, self.chunk), self.chunk)

    def near_rows(self, index):
        return self.rows(index, self.first)

    def in_copy(self, index, device):
        refs = self.refs
        return remote(
            self.near.at[:, self.near_rows(index)], refs.from_outer.at[:, self.rows(index)],
            refs.in_s, refs.in_r.at[index], device,
        )

    def mid_copy(self, index):
        refs = self.refs
        return remote(
            refs.mid_stage.at[:, self.rows(index)], refs.from_mid.at[:, self.rows(index)],
            refs.mid_s, refs.mid_r.at[index], self.place.mid_peer,
        )

    def out_copy(self, index, device):
        refs = self.refs
        return remote(
            refs.out_stage.at[:, self.rows(index)], refs.from_inner.at[:, self.rows(index)],
            refs.out_s, self.out_sem(index), device,
        )

    def out_sem(self, index):
        return self.refs.out_r if self.whole else self.refs.out_r.at[index]

    def near_options(self, index):
        return [self.near[entry, self.near_rows(index), :] for entry in range(2)]

    def forward(self, index):
        self.in_copy(index, self.place.outer_peer).wait_recv()
        rows = self.rows(index)
        refs = self.refs
        options = self.near_options(index) + [refs.from_outer[entry, rows, :] for entry in range(2)]
        for entry in range(refs.mid_stage.shape[0]):
            refs.mid_stage[entry, rows, :] = pick(options, self.routes.mid[entry])
        self.mid_copy(index).start()

    def back(self, index):
        self.mid_copy(index).wait_recv()
        rows = self.rows(index)
        refs = self.refs
        near = self.near_options(index)
        beyond = [refs.from_mid[entry, rows, :] for entry in range(refs.from_mid.shape[0])]
        for entry in range(2):
            refs.out_stage[entry, rows, :] = pick(near + beyond, self.routes.out[entry])
        self.out_copy(index, self.place.outer_peer).start()
        options = near + [refs.from_outer[entry, rows, :] for entry in range(2)] + beyond
        for entry in range(2):
            self.put(entry, self.rows(index, self.fin_first), pick(options, self.routes.inner[entry]))

    def arrive(self, index):
        if not self.whole:
            self.out_copy(index, self.place.inner_peer).wait_recv()
        rows = self.rows(index)
        options = self.near_options(index) + [self.refs.from_inner[entry, rows, :] for entry in range(2)]
        for entry in range(2):
            self.put(entry, self.rows(index, self.fin_first), pick(options, self.routes.outer[entry]))

    def send(self, first, last):
        @pl.when(self.place.is_outer)
        def _():
            @pl.loop(first, last)
            def _(index):
                self.in_copy(index, self.place.inner_peer).start()

    def go(self, forwards, backs):
        forwards = max(self.forwards, min(forwards, self.count))
        backs = max(self.backs, min(backs, forwards))

        @pl.when(self.place.is_inner)
        def _():
            pl.loop(self.forwards, forwards)(self.forward)
            pl.loop(self.backs, backs)(self.back)

        self.forwards, self.backs = forwards, backs

    def finish(self):
        ahead = self.forwards - self.backs
        first, last = self.backs, self.count - ahead

        @pl.when(self.place.is_inner)
        def _():
            @pl.loop(first, last)
            def _(index):
                self.back(index)
                self.forward(index + ahead)

        self.forwards, self.backs = self.count, last
        self.go(self.count, self.count)

    def arrivals(self):
        @pl.when(self.place.is_outer)
        def _():
            if self.whole:
                refs = self.refs
                remote(
                    refs.out_stage, refs.from_inner, refs.out_s, refs.out_r, self.place.inner_peer
                ).wait_recv()
            pl.loop(0, self.count)(self.arrive)

    def drain(self):
        refs, place = self.refs, self.place

        @pl.when(place.is_outer)
        def _():
            sent = self.near.at[:, pl.ds(self.first, self.count * self.chunk)]
            remote(sent, refs.from_outer, refs.in_s, refs.in_r.at[0], place.inner_peer).wait_send()

        @pl.when(place.is_inner)
        def _():
            remote(refs.mid_stage, refs.from_mid, refs.mid_s, refs.mid_r.at[0], place.mid_peer).wait_send()
            remote(
                refs.out_stage, refs.from_inner, refs.out_s, self.out_sem(0), place.outer_peer
            ).wait_send()


def routes_of(ps_ref, side, cap):
    slots = []
    for first, second in zip((2, 3, 0, 1, 4, 5, 6, 7), (4, 5, 6, 7, 2, 3, 0, 1)):
        slot = ps_ref[first + side * (second - first)]
        low_side = jnp.where(slot < 2, slot + 2, jnp.where(slot < 4, slot - 2, slot))
        high_side = jnp.where(slot < 2, slot + 6, jnp.where(slot < 4, slot + 2, slot - 4))
        slots.append(jnp.where(side == 0, low_side, high_side))
    crosses = lambda slot: slot >= 4
    returns = lambda slot: slot < 4
    outward = lambda slot: (slot == 2) | (slot == 3)

    def ranks(order, wanted):
        count = jnp.int32(0)
        result = {}
        for position in order:
            result[position] = count
            count = count + jnp.where(wanted(slots[position]), 1, 0)
        return result

    def source_of(places, wanted):
        found = jnp.int32(0)
        for position, place in places.items():
            found = jnp.where(wanted(position), place, found)
        return found

    send_rank = ranks((0, 1, 2, 3), crosses)
    recv_rank = ranks((4, 5, 6, 7), returns)
    out_rank = ranks((0, 1, 4, 5, 6, 7), outward)
    far_places = {position: recv_rank[position] for position in (4, 5, 6, 7)}
    mid_places = {position: position for position in range(4)}
    out_places = {0: 0, 1: 1, **{position: 2 + place for position, place in far_places.items()}}
    inner_places = {**mid_places, **{position: 4 + place for position, place in far_places.items()}}
    outer_places = {2: 0, 3: 1, **{position: 2 + rank for position, rank in out_rank.items()}}
    return types.SimpleNamespace(
        mid=[
            source_of(mid_places, lambda p: crosses(slots[p]) & (send_rank[p] == entry))
            for entry in range(cap)
        ],
        out=[
            source_of(out_places, lambda p: outward(slots[p]) & (out_rank[p] == entry))
            for entry in range(2)
        ],
        inner=[source_of(inner_places, lambda p: slots[p] == entry) for entry in range(2)],
        outer=[source_of(outer_places, lambda p: slots[p] == 2 + entry) for entry in range(2)],
    )


def kernel(cap, names, x_hbm, ps_ref, out_ref, en_ref, *scratch):
    refs = types.SimpleNamespace(**dict(zip(names, scratch)))
    own, xh, xl, rh, rl = refs.own, refs.xh, refs.xl, refs.rh, refs.rl
    rows_here = own.shape[1]
    raw_rows = refs.raw_fin.shape[1]
    row = lax.axis_index("rows")
    z = lax.axis_index("cols")
    core = row % 2
    xy = (row // 2) % XY
    zh = row // (2 * XY)
    side = z // 2
    place = types.SimpleNamespace(
        is_outer=(z % 3) == 0,
        is_inner=(z % 3) != 0,
        inner_peer={"cols": 1 + z // 3},
        outer_peer={"cols": (3 * z + 1) % 4},
        mid_peer={"cols": 3 - z},
    )
    sibling = {"rows": row + 1 - 2 * core}
    far = {"rows": (row + 2 * XY) % (4 * XY)}

    def plane_peer(step):
        return {"rows": zh * 2 * XY + ((xy + step) % XY) * 2 + core}

    def z_peer(step):
        return {"cols": (z + step) % 4}

    def greet(device):
        pl.semaphore_signal(barrier, inc=1, device_id=device, device_id_type=MESH)

    def load(pair):
        where = pl.ds(pl.multiple_of(pair * 2 * BW, 2 * BW), 2 * BW)
        return pltpu.make_async_copy(x_hbm.at[:, where], own.at[pair], refs.load_sem.at[pair])

    load(1 - core).start()
    load(core).start()
    barrier = pltpu.get_barrier_semaphore()
    greet(sibling)
    greet(far)

    @pl.loop(1, XY)
    def _(step):
        greet(plane_peer(step))

    @pl.loop(1, 4)
    def _(step):
        greet(z_peer(step))

    routes = routes_of(ps_ref, side, cap)
    raw_refs = types.SimpleNamespace(**{n[4:]: r for n, r in vars(refs).items() if n.startswith("raw_")})
    late_refs = types.SimpleNamespace(**{n[5:]: r for n, r in vars(refs).items() if n.startswith("late_")})
    raw_count = raw_rows // RAW_CHUNK
    late_count = (rows_here - raw_rows) // LATE_CHUNK
    def column(pair, half):
        return pl.ds(pl.multiple_of(pair * 2 * BW + half * BW, BW), BW)

    def put_raw(entry, rows, value):
        refs.raw_fin[entry, rows, :] = value

    def put_late(entry, rows, value):
        out_ref[rows, column(entry, 1)] = value

    raw = Stream(True, own, 0, raw_count, RAW_CHUNK, raw_refs, routes, put_raw, 0, place)
    late = Stream(False, refs.rights, 0, late_count, LATE_CHUNK, late_refs, routes, put_late, raw_rows, place)
    first_batch = RAW_FIRST[cap]

    def go_raw(forwards, backs):
        raw.go(first_batch + forwards * 2 // cap, first_batch + backs * 2 // cap)

    def go_late(forwards, backs):
        late.go(forwards * 2 // cap, backs * 2 // cap)

    def gram(pair, target):
        load(pair).wait()
        high, low = split(own[pair])
        xh[pair] = high
        xl[pair] = low
        rows = ((0,), (0,))
        cross = dot3((high[:, :BW], low[:, :BW]), (high[:, BW:], low[:, BW:]), rows)
        target[:, 0:16, :] = cross[:, :128].reshape(XY, 16, 128)
        target[:, 16:32, :] = cross[:, 128:].reshape(XY, 16, 128)
        values = own[pair]
        tile = row_of(jnp.sum(values * values, axis=0, keepdims=True))
        target[:, 32:40, :] = jnp.broadcast_to(tile[None], (XY, 8, 128))

    gmine, gsend, gpeer, rs = refs.gmine, refs.gsend, refs.gpeer, refs.rs
    gram(1 - core, gsend)
    pl.semaphore_wait(barrier, 20)
    to_sibling = remote(gsend, gpeer, refs.pair_s, refs.pair_r, sibling)
    to_sibling.start()

    gram(core, gmine)
    raw.send(0, first_batch)
    to_sibling.wait_recv()
    gmine[...] = gmine[...] + gpeer[...]

    def rs_copy(step):
        target = (xy + step) % XY
        return remote(gmine.at[target], rs.at[xy], refs.rs_s, refs.rs_r, plane_peer(step))

    def gather_copy(buffer, send, recv):
        return lambda step: remote(buffer.at[xy], buffer.at[xy], send, recv, plane_peer(step))

    def start_all(copy, last=XY):
        @pl.loop(1, last)
        def _(step):
            copy(step).start()

    def others(buffer, send, recv, device, last=XY):
        part = buffer.at[pl.ds(0, last - 1)]
        return remote(part, part, send, recv, device)

    start_all(rs_copy)
    rs[xy] = gmine[xy]

    raw.go(first_batch, 0)
    others(rs, refs.rs_s, refs.rs_r, plane_peer(1)).wait_recv()
    total = rs[0]
    for chip in range(1, XY):
        total = total + rs[chip]
    refs.zsend[...] = total
    to_far = remote(refs.zsend, refs.zrecv, refs.z_s, refs.z_r, far)
    to_far.start()
    to_far.wait_recv()
    total = refs.zsend[...] + refs.zrecv[...]
    diag_tile = total[32:40, :]
    ag, zl, fp, fag = refs.ag, refs.zl, refs.fp, refs.fag
    ag[xy] = total[0:32, :]
    zl[z] = total
    ag_copy = gather_copy(ag, refs.ag_s, refs.ag_r)
    start_all(ag_copy)

    def zl_copy(step):
        return remote(zl.at[z], zl.at[z], refs.zl_s, refs.zl_r, z_peer(step))

    start_all(zl_copy, 4)
    raw.send(first_batch, raw_count)
    go_raw(0, 0)
    go_raw(1, 0)
    others(ag, refs.ag_s, refs.ag_r, plane_peer(1)).wait_recv()

    coupling, scale = coupling_of(ag[...], diag_tile)
    coupling_parts = split(coupling)
    outer_product = dot3(coupling_parts, coupling_parts, ((1,), (1,)))
    inner_product = dot3(coupling_parts, coupling_parts, ((0,), (0,)))
    others(zl, refs.zl_s, refs.zl_r, z_peer(1), 4).wait_recv()
    fp[core] = zl[...]
    to_sibling_z = remote(zl, fp.at[core], refs.fp_s, refs.fp_r, sibling)
    to_sibling_z.start()
    fag_copy = gather_copy(fag, refs.fag_s, refs.fag_r)
    incoming_diag = []

    def gather_incoming():
        remote(zl, fp.at[1 - core], refs.fp_s, refs.fp_r, sibling).wait_recv()
        parity, plane = jnp.int32(0), jnp.int32(0)
        for pair in range(8):
            hit = ps_ref[pair] == 2 * z + core
            parity = jnp.where(hit, pair % 2, parity)
            plane = jnp.where(hit, pair // 2, plane)
        incoming = fp[parity, plane]
        fag[xy] = incoming[0:32, :]
        incoming_diag.append(incoming[32:40, :])
        start_all(fag_copy)

    def beside(sweep):
        go_raw(*((3, 0), (4, 1), (5, 2))[sweep])
        if sweep == 1:
            gather_incoming()

    go_raw(2, 0)
    left_part, right_part = polynomials(
        [outer_product, inner_product], scale, beside
    )
    rsend, rrecv = refs.rsend, refs.rrecv
    rsend[1] = right_part
    rsend[0] = dot3(split(left_part), coupling_parts)
    to_sibling_r = remote(
        rsend.at[pl.ds(0, 2)], rrecv.at[pl.ds(0, 2)], refs.ro_s.at[0], refs.ro_r.at[0], sibling
    )
    to_sibling_r.start()
    rsend[2] = left_part
    to_sibling_l = remote(rsend.at[2], rrecv.at[2], refs.ro_s.at[1], refs.ro_r.at[1], sibling)
    to_sibling_l.start()

    def spread(half, pair, blocks):
        for row_block, block in enumerate(blocks):
            high, low = split(block)
            where = (half, pair, pl.ds(row_block * BW, BW))
            rh[where] = high
            rl[where] = low

    rights = refs.rights
    esend, epeer, exy, ez = refs.esend, refs.epeer, refs.exy, refs.ez

    def rotate(half, pair, first, last):
        rows = pl.ds(first, last - first)
        result = dot3((xh[pair, rows, :], xl[pair, rows, :]), (rh[half, pair], rl[half, pair]))
        if half == 0:
            out_ref[rows, column(pair, 0)] = result
        elif first > 0:
            rights[pair] = result
        return jnp.sum(result * result, axis=0, keepdims=True)

    spread(1, core, (rsend[0], rsend[1]))
    right_sums = [rotate(1, core, raw_rows, rows_here)]
    go_raw(6, 3)
    to_sibling_r.wait_recv()
    spread(1, 1 - core, (rrecv[0], rrecv[1]))
    right_sums.append(rotate(1, 1 - core, raw_rows, rows_here))

    late.send(0, late_count)
    go_raw(raw_count, 4)
    to_sibling_l.wait_recv()
    left_sums = []

    def rotate_left(pair, source):
        spread(0, pair, (source[2], -jnp.transpose(source[0])))
        left_sums.append(rotate(0, pair, 0, rows_here))

    rotate_left(core, rsend)
    rotate_left(1 - core, rrecv)
    go_raw(raw_count, 5)
    for entry, pair in enumerate((core, 1 - core)):
        sums = right_sums[entry] + rotate(1, pair, 0, raw_rows)
        esend[pair] = row_of(jnp.concatenate([left_sums[entry], sums], 1))
    e_sibling = remote(esend, epeer, refs.e_s.at[0], refs.e_r.at[0], sibling)
    e_sibling.start()
    go_raw(raw_count, 6)
    go_late(2, 0)
    raw.go(raw_count, raw_count)

    others(fag, refs.fag_s, refs.fag_r, plane_peer(1)).wait_recv()
    fsend, frecv, fh, fl = refs.fsend, refs.frecv, refs.fh, refs.fl
    coupling, scale = coupling_of(fag[...], incoming_diag[0])
    coupling_parts = split(coupling)
    e_sibling.wait_recv()
    exy[xy] = esend[...] + epeer[...]
    exy_copy = gather_copy(exy, refs.exy_s, refs.exy_r)
    start_all(exy_copy)
    go_late(7, 0)
    inner_product = dot3(coupling_parts, coupling_parts, ((0,), (0,)))
    go_late(8, 1)
    (right_part,) = polynomials(
        [inner_product], scale, lambda sweep: go_late(*((9, 3), (11, 5), (12, 6))[sweep])
    )
    fsend[1] = right_part
    fsend[0] = dot3(coupling_parts, split(right_part))
    to_sibling_f = remote(fsend, frecv, refs.f_s, refs.f_r, sibling)
    to_sibling_f.start()
    raw.arrivals()
    go_late(14, 8)
    others(exy, refs.exy_s, refs.exy_r, plane_peer(1)).wait_recv()
    plane_sum = exy[0]
    for chip in range(1, XY):
        plane_sum = plane_sum + exy[chip]
    ez[0] = plane_sum
    e_far = remote(ez.at[0], ez.at[1], refs.e_s.at[1], refs.e_r.at[1], far)
    e_far.start()

    def finish_raw(slot, source):
        for block in range(2):
            high, low = split(source[block])
            fh[slot, pl.ds(block * BW, BW), :] = high
            fl[slot, pl.ds(block * BW, BW), :] = low
        out_ref[pl.ds(0, raw_rows), column(slot, 1)] = dot3(split(refs.raw_fin[slot]), (fh[slot], fl[slot]))

    finish_raw(core, fsend)
    go_late(17, 11)
    to_sibling_f.wait_recv()
    finish_raw(1 - core, frecv)
    late.finish()
    late.arrivals()
    e_far.wait_recv()
    energies = (ez[0] + ez[1]) / (4 * XY * rows_here)
    en_ref[0:4, :] = energies[0, 0:4, :]
    en_ref[4:8, :] = energies[1, 0:4, :]

    for copy in (to_sibling, to_sibling_r, to_sibling_l, to_sibling_z, to_sibling_f, to_far, e_sibling, e_far):
        copy.wait_send()

    for buffer, send, recv in (
        (rs, refs.rs_s, refs.rs_r), (ag, refs.ag_s, refs.ag_r), (fag, refs.fag_s, refs.fag_r), (exy, refs.exy_s, refs.exy_r)
    ):
        others(buffer, send, recv, plane_peer(1)).wait_send()
    others(zl, refs.zl_s, refs.zl_r, z_peer(1), 4).wait_send()
    raw.drain()
    late.drain()


def call(cap, snapshots, partner_slot):
    rows = snapshots.shape[0]
    raw_rows = RAW_ROWS[cap]
    dma = pltpu.SemaphoreType.DMA
    f32 = lambda *shape: pltpu.VMEM(shape, F32)
    b16 = lambda *shape: pltpu.VMEM(shape, BF16)
    scratch = dict(
        own=f32(2, rows, 2 * BW), xh=b16(2, rows, 2 * BW), xl=b16(2, rows, 2 * BW),
        rh=b16(2, 2, 2 * BW, BW), rl=b16(2, 2, 2 * BW, BW),
        rights=f32(2, rows - raw_rows, BW),
        gmine=f32(XY, 40, 128), gsend=f32(XY, 40, 128), gpeer=f32(XY, 40, 128), rs=f32(XY, 40, 128),
        zsend=f32(40, 128), zrecv=f32(40, 128), ag=f32(XY, 32, 128),
        zl=f32(4, 40, 128), fp=f32(2, 4, 40, 128), fag=f32(XY, 32, 128),
        rsend=f32(3, BW, BW), rrecv=f32(3, BW, BW),
        fsend=f32(2, BW, BW), frecv=f32(2, BW, BW), fh=b16(2, 2 * BW, BW), fl=b16(2, 2 * BW, BW),
        esend=f32(2, 8, 128), epeer=f32(2, 8, 128), exy=f32(XY, 2, 8, 128), ez=f32(2, 2, 8, 128),
        load_sem=dma((2,)), pair_s=dma, pair_r=dma, rs_s=dma, rs_r=dma,
        z_s=dma, z_r=dma, ag_s=dma, ag_r=dma, zl_s=dma, zl_r=dma,
        fp_s=dma, fp_r=dma, fag_s=dma, fag_r=dma, ro_s=dma((2,)), ro_r=dma((2,)), f_s=dma, f_r=dma,
        e_s=dma((2,)), e_r=dma((2,)), exy_s=dma, exy_r=dma,
        raw_fin=f32(2, raw_rows, 2 * BW),
    )
    for name, height, width, chunk in (
        ("raw", raw_rows, 2 * BW, RAW_CHUNK), ("late", rows - raw_rows, BW, LATE_CHUNK)
    ):
        for buffer, blocks in (("mid_stage", cap), ("from_mid", cap), ("out_stage", 2), ("from_outer", 2), ("from_inner", 2)):
            scratch[f"{name}_{buffer}"] = f32(blocks, height, width)
        for sem in ("in_s", "mid_s", "out_s"):
            scratch[f"{name}_{sem}"] = dma
        for sem in ("in_r", "mid_r", "out_r"):
            scratch[f"{name}_{sem}"] = dma((height // chunk,))
    scratch["raw_out_r"] = dma
    return pl.pallas_call(
        functools.partial(kernel, cap, tuple(scratch)),
        out_shape=(
            jax.ShapeDtypeStruct(snapshots.shape, F32),
            jax.ShapeDtypeStruct((8, 128), F32),
        ),
        in_specs=[pl.BlockSpec(memory_space=pl.ANY), pl.BlockSpec(memory_space=pltpu.SMEM)],
        out_specs=(pl.BlockSpec(memory_space=pltpu.VMEM), pl.BlockSpec(memory_space=pltpu.VMEM)),
        scratch_shapes=list(scratch.values()),
        name=f"round_{cap}",
        compiler_params=pltpu.CompilerParams(
            collective_id=cap, has_side_effects=True, vmem_limit_bytes=48 << 20
        ),
    )(snapshots, partner_slot)


def on_device(snapshots, partner_slot):
    crossing = jnp.sum((partner_slot[:4] >= 4).astype(jnp.int32))
    moved, energies = lax.switch(
        jnp.maximum(crossing, 2) - 2,
        [functools.partial(call, cap) for cap in (2, 3, 4)],
        snapshots,
        partner_slot,
    )
    return moved, energies.reshape(-1)


def solution(mesh):
    in_specs = (P("rows", "cols"), P())
    out_specs = (P("rows", "cols"), P("cols"))
    return jax.shard_map(
        on_device, mesh=mesh, in_specs=in_specs, out_specs=out_specs, check_vma=False
    )
```

time: 1110 us -> 67.5 us (0.06)
  the two profiles are of different devices: /device:TPU:32 before, /device:TPU:1 now
where the time goes in v2:
time: 67.5 us; the launch traced here: 67.3 us
  Pallas kernels  62.6 us (93%)
  local copies, waits for them, and re-layouts  1.91 us (3%)
  other arithmetic  1.29 us (2%)
  between operations  1.29 us (2%)
    pallas_call x1, Pallas kernels, call(): pl.pallas_call(functools.partial(kernel, cap, tuple(scratch)), out_shape=...  62.6 us
    unnamed x2, local copies, waits for them, and re-layouts  1.91 us

profile of v2, /device:TPU:1, one launch (start us, length us, event | category | flops | bytes accessed | tf_op | source)
XLA Modules:
  0.0 67.3 jit_solution(6367939905715125008)
XLA Ops:
  0.6 1.3 %fusion = s32[]{:T(128)} fusion(s32[8]{0:T(128)} %param.6), kind=kLoop, calls=%fused_computation.1 | loop fusion | flops 11 | bytes 20 | tf_op jit(solution)/shard_map/reduce_sum | solution.py:611
  2.6 62.8 %conditional.1 = (f32[512,1024]{1,0:T(8,128)S(1)}, f32[1024]{0:T(1024)S(1)}) conditional(s32[]{:T(128)} %clamp.3, (f32[512,1024]{1,0:T(8,128)}, s32[8]{0:T(128)}) %tuple.22, (f32[512,1024]{1,0:T(8,128)}, s32[8]{0:T(128)}) %tuple.22, (f32[512,1024]{1,0:T(8,128)}, s32[8]{0:T(128)}) %tuple.22), branch_computations={%region_1.0_spmd, %region_2.0_spmd, %region_3.0_spmd} | conditional | bytes 16 | solution.py:612
  2.6 62.6 %round_2.1 = (f32[512,1024]{1,0:T(8,128)S(1)}, f32[8,128]{1,0:T(8,128)S(1)}) custom-call(f32[512,1024]{1,0:T(8,128)} %get-tuple-element.37.x_hbm, s32[8]{0:T(128)} %get-tuple-element.20.ps_ref), custom_call_target="tpu_custom_call" | custom-call | tf_op jit(solution)/shard_map/cond/branch_0_fun/round_2/pallas_call | solution.py:594
  65.4 1.3 %copy.18 = f32[512,1024]{1,0:T(8,128)} copy(f32[512,1024]{1,0:T(8,128)S(1)} %get-tuple-element.48) | data formatting | bytes 4194304
  66.7 0.6 copy.19

commit v3 on v2

--- a/solution.py
+++ b/solution.py
@@ -17,7 +17,8 @@
 RAW_CHUNK = 16
 LATE_CHUNK = 16
 RAW_FIRST = {2: 4, 3: 3, 4: 2}
-RAW_ROWS = {2: 192, 3: 128, 4: 96}
+RAW_SENT = {2: 7, 3: 4, 4: 3}
+RAW_ROWS = {2: 224, 3: 128, 4: 96}
 
 
 def split(value):
@@ -270,7 +271,7 @@
     )
 
 
-def kernel(cap, names, x_hbm, ps_ref, out_ref, en_ref, *scratch):
+def kernel(cap, names, x_hbm, ps_any, out_ref, en_ref, *scratch):
     refs = types.SimpleNamespace(**dict(zip(names, scratch)))
     own, xh, xl, rh, rl = refs.own, refs.xh, refs.xl, refs.rh, refs.rl
     rows_here = own.shape[1]
@@ -306,6 +307,9 @@
 
     load(1 - core).start()
     load(core).start()
+    ps_ref = refs.slots
+    ps_load = pltpu.make_async_copy(ps_any, ps_ref, refs.ps_sem)
+    ps_load.start()
     barrier = pltpu.get_barrier_semaphore()
     greet(sibling)
     greet(far)
@@ -318,7 +322,7 @@
     def _(step):
         greet(z_peer(step))
 
-    routes = routes_of(ps_ref, side, cap)
+    routes = types.SimpleNamespace()
     raw_refs = types.SimpleNamespace(**{n[4:]: r for n, r in vars(refs).items() if n.startswith("raw_")})
     late_refs = types.SimpleNamespace(**{n[5:]: r for n, r in vars(refs).items() if n.startswith("late_")})
     raw_count = raw_rows // RAW_CHUNK
@@ -335,6 +339,7 @@
     raw = Stream(True, own, 0, raw_count, RAW_CHUNK, raw_refs, routes, put_raw, 0, place)
     late = Stream(False, refs.rights, 0, late_count, LATE_CHUNK, late_refs, routes, put_late, raw_rows, place)
     first_batch = RAW_FIRST[cap]
+    first_sent = RAW_SENT[cap]
 
     def go_raw(forwards, backs):
         raw.go(first_batch + forwards * 2 // cap, first_batch + backs * 2 // cap)
@@ -362,7 +367,7 @@
     to_sibling.start()
 
     gram(core, gmine)
-    raw.send(0, first_batch)
+    raw.send(0, first_sent)
     to_sibling.wait_recv()
     gmine[...] = gmine[...] + gpeer[...]
 
@@ -385,6 +390,8 @@
     start_all(rs_copy)
     rs[xy] = gmine[xy]
 
+    ps_load.wait()
+    vars(routes).update(vars(routes_of(ps_ref, side, cap)))
     raw.go(first_batch, 0)
     others(rs, refs.rs_s, refs.rs_r, plane_peer(1)).wait_recv()
     total = rs[0]
@@ -406,12 +413,13 @@
         return remote(zl.at[z], zl.at[z], refs.zl_s, refs.zl_r, z_peer(step))
 
     start_all(zl_copy, 4)
-    raw.send(first_batch, raw_count)
-    go_raw(0, 0)
-    go_raw(1, 0)
+    raw.send(first_sent, raw_count)
+    go_raw(2, 0)
+    go_raw(3, 1)
     others(ag, refs.ag_s, refs.ag_r, plane_peer(1)).wait_recv()
 
     coupling, scale = coupling_of(ag[...], diag_tile)
+    go_raw(4, 2)
     coupling_parts = split(coupling)
     outer_product = dot3(coupling_parts, coupling_parts, ((1,), (1,)))
     inner_product = dot3(coupling_parts, coupling_parts, ((0,), (0,)))
@@ -435,11 +443,9 @@
         start_all(fag_copy)
 
     def beside(sweep):
-        go_raw(*((3, 0), (4, 1), (5, 2))[sweep])
-        if sweep == 1:
-            gather_incoming()
-
-    go_raw(2, 0)
+        go_raw(*((5, 3), (6, 3), (7, 4))[sweep])
+
+    go_raw(5, 2)
     left_part, right_part = polynomials(
         [outer_product, inner_product], scale, beside
     )
@@ -475,13 +481,15 @@
 
     spread(1, core, (rsend[0], rsend[1]))
     right_sums = [rotate(1, core, raw_rows, rows_here)]
-    go_raw(6, 3)
+    go_raw(9, 5)
+    gather_incoming()
+    go_raw(10, 6)
     to_sibling_r.wait_recv()
     spread(1, 1 - core, (rrecv[0], rrecv[1]))
     right_sums.append(rotate(1, 1 - core, raw_rows, rows_here))
 
     late.send(0, late_count)
-    go_raw(raw_count, 4)
+    go_raw(raw_count, 7)
     to_sibling_l.wait_recv()
     left_sums = []
 
@@ -490,14 +498,15 @@
         left_sums.append(rotate(0, pair, 0, rows_here))
 
     rotate_left(core, rsend)
+    go_raw(raw_count, 8)
     rotate_left(1 - core, rrecv)
-    go_raw(raw_count, 5)
+    go_raw(raw_count, 9)
     for entry, pair in enumerate((core, 1 - core)):
         sums = right_sums[entry] + rotate(1, pair, 0, raw_rows)
         esend[pair] = row_of(jnp.concatenate([left_sums[entry], sums], 1))
     e_sibling = remote(esend, epeer, refs.e_s.at[0], refs.e_r.at[0], sibling)
     e_sibling.start()
-    go_raw(raw_count, 6)
+    go_raw(raw_count, 9)
     go_late(2, 0)
     raw.go(raw_count, raw_count)
 
@@ -575,7 +584,7 @@
         rsend=f32(3, BW, BW), rrecv=f32(3, BW, BW),
         fsend=f32(2, BW, BW), frecv=f32(2, BW, BW), fh=b16(2, 2 * BW, BW), fl=b16(2, 2 * BW, BW),
         esend=f32(2, 8, 128), epeer=f32(2, 8, 128), exy=f32(XY, 2, 8, 128), ez=f32(2, 2, 8, 128),
-        load_sem=dma((2,)), pair_s=dma, pair_r=dma, rs_s=dma, rs_r=dma,
+        slots=pltpu.SMEM((8,), jnp.int32), ps_sem=dma, load_sem=dma((2,)), pair_s=dma, pair_r=dma, rs_s=dma, rs_r=dma,
         z_s=dma, z_r=dma, ag_s=dma, ag_r=dma, zl_s=dma, zl_r=dma,
         fp_s=dma, fp_r=dma, fag_s=dma, fag_r=dma, ro_s=dma((2,)), ro_r=dma((2,)), f_s=dma, f_r=dma,
         e_s=dma((2,)), e_r=dma((2,)), exy_s=dma, exy_r=dma,
@@ -597,7 +606,7 @@
             jax.ShapeDtypeStruct(snapshots.shape, F32),
             jax.ShapeDtypeStruct((8, 128), F32),
         ),
-        in_specs=[pl.BlockSpec(memory_space=pl.ANY), pl.BlockSpec(memory_space=pltpu.SMEM)],
+        in_specs=[pl.BlockSpec(memory_space=pl.ANY)] * 2,
         out_specs=(pl.BlockSpec(memory_space=pltpu.VMEM), pl.BlockSpec(memory_space=pltpu.VMEM)),
         scratch_shapes=list(scratch.values()),
         name=f"round_{cap}",
@@ -607,6 +616,18 @@
     )(snapshots, partner_slot)
 
 
+def hand_out(moved_ref, energies_ref, out_ref, en_ref, sems):
+    rows = moved_ref.shape[0] // 4
+    copies = [pltpu.make_async_copy(energies_ref, en_ref, sems.at[4])]
+    for part in range(4):
+        where = pl.ds(part * rows, rows)
+        copies.append(pltpu.make_async_copy(moved_ref.at[where], out_ref.at[where], sems.at[part]))
+    for copy in copies:
+        copy.start()
+    for copy in copies:
+        copy.wait()
+
+
 def on_device(snapshots, partner_slot):
     crossing = jnp.sum((partner_slot[:4] >= 4).astype(jnp.int32))
     moved, energies = lax.switch(
@@ -615,6 +636,18 @@
         snapshots,
         partner_slot,
     )
+    anywhere = pl.BlockSpec(memory_space=pl.ANY)
+    moved, energies = pl.pallas_call(
+        hand_out,
+        out_shape=(
+            jax.ShapeDtypeStruct(moved.shape, F32),
+            jax.ShapeDtypeStruct(energies.shape, F32),
+        ),
+        in_specs=[anywhere, anywhere],
+        out_specs=(anywhere, anywhere),
+        scratch_shapes=[pltpu.SemaphoreType.DMA((5,))],
+        name="hand_out",
+    )(moved, energies)
     return moved, energies.reshape(-1)
 
 

time: 67.5 us -> 65.1 us (0.964)
  local copies, waits for them, and re-layouts: 1.91 us -> 0 us
    pallas_call x1, Pallas kernels: 62.6 us -> 60.6 us  [call(): pl.pallas_call(functools.partial(kernel, cap, tuple(scratch)), out_shape=...]
    unnamed x2 -> x0, local copies, waits for them, and re-layouts: 1.91 us -> none
    pallas_call x0 -> x1, Pallas kernels: none -> 1.36 us  [on_device(): pl.pallas_call(hand_out, out_shape=(jax.ShapeDtypeStruct(moved.shape, F32...]
where the time goes in v3:
time: 65.1 us; the launch traced here: 65 us
  Pallas kernels  62 us (95%)
  between operations  1.47 us (2%)
  other arithmetic  1.29 us (2%)
    pallas_call x1, Pallas kernels, call(): pl.pallas_call(functools.partial(kernel, cap, tuple(scratch)), out_shape=...  60.6 us
    pallas_call x1, Pallas kernels, on_device(): pl.pallas_call(hand_out, out_shape=(jax.ShapeDtypeStruct(moved.shape, F32...  1.36 us

profile of v3, /device:TPU:1, one launch (start us, length us, event | category | flops | bytes accessed | tf_op | source)
XLA Modules:
  0.0 65.0 jit_solution(16865177004567326570)
XLA Ops:
  0.6 1.3 %fusion = s32[]{:T(128)} fusion(s32[8]{0:T(128)} %param.6), kind=kLoop, calls=%fused_computation.1 | loop fusion | flops 11 | bytes 20 | tf_op jit(solution)/shard_map/reduce_sum | solution.py:632
  2.6 60.9 %conditional.1 = ((f32[512,1024]{1,0:T(8,128)S(1)}, f32[8,128]{1,0:T(8,128)S(1)})) conditional(s32[]{:T(128)} %clamp.3, (f32[512,1024]{1,0:T(8,128)}, s32[8]{0:T(128)}) %tuple.17, (f32[512,1024]{1,0:T(8,128)}, s32[8]{0:T(128)}) %tuple.17, (f32[512,1024]{1,0:T(8,128)}, s32[8]{0:T(128)}) %tuple.17), branch_computations={%region_1.0_spmd, %region_2.0_spmd, %region_3.0_spmd} | conditional | bytes 8 | solution.py:633
  2.6 60.6 %round_2.1 = (f32[512,1024]{1,0:T(8,128)S(1)}, f32[8,128]{1,0:T(8,128)S(1)}) custom-call(f32[512,1024]{1,0:T(8,128)} %get-tuple-element.12.x_hbm, s32[8]{0:T(128)} %get-tuple-element.13.ps_any), custom_call_target="tpu_custom_call" | custom-call | tf_op jit(solution)/shard_map/cond/branch_0_fun/round_2/pallas_call | solution.py:603
  63.5 1.4 %hand_out.1 = (f32[512,1024]{1,0:T(8,128)}, f32[8,128]{1,0:T(8,128)}) custom-call(f32[512,1024]{1,0:T(8,128)S(1)} %get-tuple-element.24.moved_ref, f32[8,128]{1,0:T(8,128)S(1)} %get-tuple-element.25.energies_ref), custom_call_target="tpu_custom_call" | custom-call | tf_op jit(solution)/shard_map/hand_out/pallas_call | solution.py:640

commit v4 on v3

--- a/solution.py
+++ b/solution.py
@@ -16,9 +16,10 @@
 XY = 16
 RAW_CHUNK = 16
 LATE_CHUNK = 16
+EARLY = 6
 RAW_FIRST = {2: 4, 3: 3, 4: 2}
-RAW_SENT = {2: 7, 3: 4, 4: 3}
-RAW_ROWS = {2: 224, 3: 128, 4: 96}
+RAW_SENT = {2: 7, 3: 5, 4: 4}
+RAW_ROWS = {2: 208, 3: 144, 4: 128}
 
 
 def split(value):
@@ -58,23 +59,36 @@
     eye = (
         lax.broadcasted_iota(jnp.int32, (BW, BW), 0) == lax.broadcasted_iota(jnp.int32, (BW, BW), 1)
     ).astype(F32)
-    squares = [(eye + start) * (scale * scale) for start in starts]
-    totals = []
-    for sweep in range(SWEEPS):
-        steps = [1.5 * eye - 0.5 * square for square in squares]
-        step_parts = [split(step) for step in steps]
-        if sweep == 0:
-            totals = [scale * step for step in steps]
-            halves = [dot3(split(square), step) for square, step in zip(squares, step_parts)]
-        elif sweep == SWEEPS - 1:
-            return [dot3(split(total), step) for total, step in zip(totals, step_parts)]
+
+    def times(uppers, lowers, rights):
+        stacks = [jnp.concatenate(parts, 0) for parts in zip(uppers, lowers)]
+        results = [dot3(split(stack), split(right)) for stack, right in zip(stacks, rights)]
+        return [result[:BW] for result in results], [result[BW:] for result in results]
+
+    firsts = [(eye + start) * (scale * scale) for start in starts]
+    parts = [split(first) for first in firsts]
+    powers = [dot3(part, part) for part in parts]
+    squares, crossed = times(
+        [0.25 * first - 1.5 * eye for first in firsts],
+        [1.125 * first - 0.125 * power for first, power in zip(firsts, powers)],
+        powers,
+    )
+    squares = [square + 2.25 * first for square, first in zip(squares, firsts)]
+    totals = [
+        scale * (2.25 * eye - 2.4375 * first + 1.6875 * power - 0.5 * cross)
+        for first, power, cross in zip(firsts, powers, crossed)
+    ]
+    for sweep in range(2, SWEEPS):
+        between(2 * sweep - 4)
+        powers, crossed = times(squares, totals, squares)
+        factors = [2.25 * eye - 1.5 * square + 0.25 * power for square, power in zip(squares, powers)]
+        if sweep < SWEEPS - 1:
+            between(1)
+            squares, crossed = times(squares, crossed, factors)
         else:
-            stacks = [jnp.concatenate(parts, 0) for parts in zip(totals, squares)]
-            stacks = [dot3(split(stack), step) for stack, step in zip(stacks, step_parts)]
-            totals = [stack[:BW] for stack in stacks]
-            halves = [stack[BW:] for stack in stacks]
-        squares = [dot3(split(half), step) for half, step in zip(halves, step_parts)]
-        between(sweep)
+            crossed = [dot3(split(cross), split(factor)) for cross, factor in zip(crossed, factors)]
+        totals = [1.5 * total - 0.5 * cross for total, cross in zip(totals, crossed)]
+    return totals
 
 
 def pick(options, index):
@@ -172,6 +186,18 @@
             @pl.loop(first, last)
             def _(index):
                 self.in_copy(index, self.place.inner_peer).start()
+
+    def send_slot(self, slot, first, last):
+        refs = self.refs
+
+        @pl.when(self.place.is_outer)
+        def _():
+            @pl.loop(first, last)
+            def _(index):
+                remote(
+                    self.near.at[slot, self.near_rows(index)], refs.from_outer.at[slot, self.rows(index)],
+                    refs.in_s, refs.in_r.at[index], self.place.inner_peer,
+                ).start()
 
     def go(self, forwards, backs):
         forwards = max(self.forwards, min(forwards, self.count))
@@ -362,11 +388,11 @@
 
     gmine, gsend, gpeer, rs = refs.gmine, refs.gsend, refs.gpeer, refs.rs
     gram(1 - core, gsend)
+    gram(core, gmine)
     pl.semaphore_wait(barrier, 20)
     to_sibling = remote(gsend, gpeer, refs.pair_s, refs.pair_r, sibling)
     to_sibling.start()
 
-    gram(core, gmine)
     raw.send(0, first_sent)
     to_sibling.wait_recv()
     gmine[...] = gmine[...] + gpeer[...]
@@ -420,6 +446,10 @@
 
     coupling, scale = coupling_of(ag[...], diag_tile)
     go_raw(4, 2)
+    rsend, rrecv = refs.rsend, refs.rrecv
+    rsend[0] = coupling
+    to_sibling_k = remote(rsend.at[0], rrecv.at[0], refs.ro_s.at[2], refs.ro_r.at[2], sibling)
+    to_sibling_k.start()
     coupling_parts = split(coupling)
     outer_product = dot3(coupling_parts, coupling_parts, ((1,), (1,)))
     inner_product = dot3(coupling_parts, coupling_parts, ((0,), (0,)))
@@ -449,12 +479,8 @@
     left_part, right_part = polynomials(
         [outer_product, inner_product], scale, beside
     )
-    rsend, rrecv = refs.rsend, refs.rrecv
     rsend[1] = right_part
-    rsend[0] = dot3(split(left_part), coupling_parts)
-    to_sibling_r = remote(
-        rsend.at[pl.ds(0, 2)], rrecv.at[pl.ds(0, 2)], refs.ro_s.at[0], refs.ro_r.at[0], sibling
-    )
+    to_sibling_r = remote(rsend.at[1], rrecv.at[1], refs.ro_s.at[0], refs.ro_r.at[0], sibling)
     to_sibling_r.start()
     rsend[2] = left_part
     to_sibling_l = remote(rsend.at[2], rrecv.at[2], refs.ro_s.at[1], refs.ro_r.at[1], sibling)
@@ -479,57 +505,66 @@
             rights[pair] = result
         return jnp.sum(result * result, axis=0, keepdims=True)
 
-    spread(1, core, (rsend[0], rsend[1]))
+    def across_of(source, entry):
+        return dot3(split(source[0]), split(source[entry]))
+
+    acrosses = [across_of(rsend, 1)]
+    spread(1, core, (acrosses[0], right_part))
     right_sums = [rotate(1, core, raw_rows, rows_here)]
+    late.send_slot(core, 0, EARLY)
     go_raw(9, 5)
     gather_incoming()
     go_raw(10, 6)
+    to_sibling_k.wait_recv()
     to_sibling_r.wait_recv()
-    spread(1, 1 - core, (rrecv[0], rrecv[1]))
+    acrosses.append(across_of(rrecv, 1))
+    spread(1, 1 - core, (acrosses[1], rrecv[1]))
     right_sums.append(rotate(1, 1 - core, raw_rows, rows_here))
 
-    late.send(0, late_count)
+    late.send_slot(1 - core, 0, EARLY)
+    late.send(EARLY, late_count)
     go_raw(raw_count, 7)
     to_sibling_l.wait_recv()
     left_sums = []
 
     def rotate_left(pair, source):
-        spread(0, pair, (source[2], -jnp.transpose(source[0])))
+        spread(0, pair, (source[2], -jnp.transpose(acrosses[len(left_sums)])))
         left_sums.append(rotate(0, pair, 0, rows_here))
 
     rotate_left(core, rsend)
     go_raw(raw_count, 8)
     rotate_left(1 - core, rrecv)
     go_raw(raw_count, 9)
+    go_late(1, 0)
     for entry, pair in enumerate((core, 1 - core)):
         sums = right_sums[entry] + rotate(1, pair, 0, raw_rows)
         esend[pair] = row_of(jnp.concatenate([left_sums[entry], sums], 1))
     e_sibling = remote(esend, epeer, refs.e_s.at[0], refs.e_r.at[0], sibling)
     e_sibling.start()
     go_raw(raw_count, 9)
-    go_late(2, 0)
+    go_late(3, 0)
     raw.go(raw_count, raw_count)
 
     others(fag, refs.fag_s, refs.fag_r, plane_peer(1)).wait_recv()
     fsend, frecv, fh, fl = refs.fsend, refs.frecv, refs.fh, refs.fl
     coupling, scale = coupling_of(fag[...], incoming_diag[0])
     coupling_parts = split(coupling)
+    go_late(5, 0)
+    inner_product = dot3(coupling_parts, coupling_parts, ((0,), (0,)))
     e_sibling.wait_recv()
     exy[xy] = esend[...] + epeer[...]
     exy_copy = gather_copy(exy, refs.exy_s, refs.exy_r)
     start_all(exy_copy)
-    go_late(7, 0)
-    inner_product = dot3(coupling_parts, coupling_parts, ((0,), (0,)))
     go_late(8, 1)
     (right_part,) = polynomials(
-        [inner_product], scale, lambda sweep: go_late(*((9, 3), (11, 5), (12, 6))[sweep])
+        [inner_product], scale, lambda sweep: go_late(*((9, 2), (11, 3), (12, 5))[sweep])
     )
     fsend[1] = right_part
     fsend[0] = dot3(coupling_parts, split(right_part))
     to_sibling_f = remote(fsend, frecv, refs.f_s, refs.f_r, sibling)
     to_sibling_f.start()
     raw.arrivals()
-    go_late(14, 8)
+    go_late(14, 7)
     others(exy, refs.exy_s, refs.exy_r, plane_peer(1)).wait_recv()
     plane_sum = exy[0]
     for chip in range(1, XY):
@@ -546,7 +581,7 @@
         out_ref[pl.ds(0, raw_rows), column(slot, 1)] = dot3(split(refs.raw_fin[slot]), (fh[slot], fl[slot]))
 
     finish_raw(core, fsend)
-    go_late(17, 11)
+    go_late(16, 9)
     to_sibling_f.wait_recv()
     finish_raw(1 - core, frecv)
     late.finish()
@@ -556,7 +591,7 @@
     en_ref[0:4, :] = energies[0, 0:4, :]
     en_ref[4:8, :] = energies[1, 0:4, :]
 
-    for copy in (to_sibling, to_sibling_r, to_sibling_l, to_sibling_z, to_sibling_f, to_far, e_sibling, e_far):
+    for copy in (to_sibling, to_sibling_k, to_sibling_r, to_sibling_l, to_sibling_z, to_sibling_f, to_far, e_sibling, e_far):
         copy.wait_send()
 
     for buffer, send, recv in (
@@ -586,7 +621,7 @@
         esend=f32(2, 8, 128), epeer=f32(2, 8, 128), exy=f32(XY, 2, 8, 128), ez=f32(2, 2, 8, 128),
         slots=pltpu.SMEM((8,), jnp.int32), ps_sem=dma, load_sem=dma((2,)), pair_s=dma, pair_r=dma, rs_s=dma, rs_r=dma,
         z_s=dma, z_r=dma, ag_s=dma, ag_r=dma, zl_s=dma, zl_r=dma,
-        fp_s=dma, fp_r=dma, fag_s=dma, fag_r=dma, ro_s=dma((2,)), ro_r=dma((2,)), f_s=dma, f_r=dma,
+        fp_s=dma, fp_r=dma, fag_s=dma, fag_r=dma, ro_s=dma((3,)), ro_r=dma((3,)), f_s=dma, f_r=dma,
         e_s=dma((2,)), e_r=dma((2,)), exy_s=dma, exy_r=dma,
         raw_fin=f32(2, raw_rows, 2 * BW),
     )

time: 65.1 us -> 64.9 us (level)
  no operation moved by 1% of the time
where the time goes in v4:
time: 64.9 us; the launch traced here: 64.8 us
  Pallas kernels  61.7 us (95%)
  between operations  1.47 us (2%)
  other arithmetic  1.29 us (2%)
    pallas_call x1, Pallas kernels, call(): pl.pallas_call(functools.partial(kernel, cap, tuple(scratch)), out_shape=...  60.4 us
    pallas_call x1, Pallas kernels, on_device(): pl.pallas_call(hand_out, out_shape=(jax.ShapeDtypeStruct(moved.shape, F32...  1.36 us

profile of v4, /device:TPU:1, one launch (start us, length us, event | category | flops | bytes accessed | tf_op | source)
XLA Modules:
  0.0 64.8 jit_solution(16365106645637224953)
XLA Ops:
  0.6 1.3 %fusion = s32[]{:T(128)} fusion(s32[8]{0:T(128)} %param.6), kind=kLoop, calls=%fused_computation.1 | loop fusion | flops 11 | bytes 20 | tf_op jit(solution)/shard_map/reduce_sum | solution.py:667
  2.6 60.6 %conditional.1 = ((f32[512,1024]{1,0:T(8,128)S(1)}, f32[8,128]{1,0:T(8,128)S(1)})) conditional(s32[]{:T(128)} %clamp.3, (f32[512,1024]{1,0:T(8,128)}, s32[8]{0:T(128)}) %tuple.17, (f32[512,1024]{1,0:T(8,128)}, s32[8]{0:T(128)}) %tuple.17, (f32[512,1024]{1,0:T(8,128)}, s32[8]{0:T(128)}) %tuple.17), branch_computations={%region_1.0_spmd, %region_2.0_spmd, %region_3.0_spmd} | conditional | bytes 8 | solution.py:668
  2.6 60.4 %round_2.1 = (f32[512,1024]{1,0:T(8,128)S(1)}, f32[8,128]{1,0:T(8,128)S(1)}) custom-call(f32[512,1024]{1,0:T(8,128)} %get-tuple-element.12.x_hbm, s32[8]{0:T(128)} %get-tuple-element.13.ps_any), custom_call_target="tpu_custom_call" | custom-call | tf_op jit(solution)/shard_map/cond/branch_0_fun/round_2/pallas_call | solution.py:638
  63.2 1.4 %hand_out.1 = (f32[512,1024]{1,0:T(8,128)}, f32[8,128]{1,0:T(8,128)}) custom-call(f32[512,1024]{1,0:T(8,128)S(1)} %get-tuple-element.24.moved_ref, f32[8,128]{1,0:T(8,128)S(1)} %get-tuple-element.25.energies_ref), custom_call_target="tpu_custom_call" | custom-call | tf_op jit(solution)/shard_map/hand_out/pallas_call | solution.py:675

commit v5 on v4

--- a/solution.py
+++ b/solution.py
@@ -18,7 +18,8 @@
 LATE_CHUNK = 16
 EARLY = 6
 RAW_FIRST = {2: 4, 3: 3, 4: 2}
-RAW_SENT = {2: 7, 3: 5, 4: 4}
+RAW_SENT = {2: 6, 3: 5, 4: 4}
+RAW_BACK = {2: 3, 3: 1, 4: 1}
 RAW_ROWS = {2: 208, 3: 144, 4: 128}
 
 
@@ -426,6 +427,7 @@
     refs.zsend[...] = total
     to_far = remote(refs.zsend, refs.zrecv, refs.z_s, refs.z_r, far)
     to_far.start()
+    raw.go(first_batch, RAW_BACK[cap])
     to_far.wait_recv()
     total = refs.zsend[...] + refs.zrecv[...]
     diag_tile = total[32:40, :]

time: 64.9 us -> 66.1 us (1.018)
  Pallas kernels: 61.7 us -> 63 us
    pallas_call x1, Pallas kernels: 60.4 us -> 61.6 us  [call(): pl.pallas_call(functools.partial(kernel, cap, tuple(scratch)), out_shape=...]
where the time goes in v5:
time: 66.1 us; the launch traced here: 66 us
  Pallas kernels  63 us (95%)
  between operations  1.47 us (2%)
  other arithmetic  1.29 us (2%)
    pallas_call x1, Pallas kernels, call(): pl.pallas_call(functools.partial(kernel, cap, tuple(scratch)), out_shape=...  61.6 us
    pallas_call x1, Pallas kernels, on_device(): pl.pallas_call(hand_out, out_shape=(jax.ShapeDtypeStruct(moved.shape, F32...  1.36 us

profile of v5, /device:TPU:1, one launch (start us, length us, event | category | flops | bytes accessed | tf_op | source)
XLA Modules:
  0.0 66.0 jit_solution(8749853243281655713)
XLA Ops:
  0.6 1.3 %fusion = s32[]{:T(128)} fusion(s32[8]{0:T(128)} %param.6), kind=kLoop, calls=%fused_computation.1 | loop fusion | flops 11 | bytes 20 | tf_op jit(solution)/shard_map/reduce_sum | solution.py:669
  2.6 61.9 %conditional.1 = ((f32[512,1024]{1,0:T(8,128)S(1)}, f32[8,128]{1,0:T(8,128)S(1)})) conditional(s32[]{:T(128)} %clamp.3, (f32[512,1024]{1,0:T(8,128)}, s32[8]{0:T(128)}) %tuple.17, (f32[512,1024]{1,0:T(8,128)}, s32[8]{0:T(128)}) %tuple.17, (f32[512,1024]{1,0:T(8,128)}, s32[8]{0:T(128)}) %tuple.17), branch_computations={%region_1.0_spmd, %region_2.0_spmd, %region_3.0_spmd} | conditional | bytes 8 | solution.py:670
  2.6 61.6 %round_2.1 = (f32[512,1024]{1,0:T(8,128)S(1)}, f32[8,128]{1,0:T(8,128)S(1)}) custom-call(f32[512,1024]{1,0:T(8,128)} %get-tuple-element.12.x_hbm, s32[8]{0:T(128)} %get-tuple-element.13.ps_any), custom_call_target="tpu_custom_call" | custom-call | tf_op jit(solution)/shard_map/cond/branch_0_fun/round_2/pallas_call | solution.py:640
  64.5 1.4 %hand_out.1 = (f32[512,1024]{1,0:T(8,128)}, f32[8,128]{1,0:T(8,128)}) custom-call(f32[512,1024]{1,0:T(8,128)S(1)} %get-tuple-element.24.moved_ref, f32[8,128]{1,0:T(8,128)S(1)} %get-tuple-element.25.energies_ref), custom_call_target="tpu_custom_call" | custom-call | tf_op jit(solution)/shard_map/hand_out/pallas_call | solution.py:677

commit v6 on v4

--- a/solution.py
+++ b/solution.py
@@ -503,6 +503,7 @@
             out_ref[rows, column(pair, 0)] = result
         elif first > 0:
             rights[pair] = result
+            return None
         return jnp.sum(result * result, axis=0, keepdims=True)
 
     def across_of(source, entry):
@@ -510,7 +511,7 @@
 
     acrosses = [across_of(rsend, 1)]
     spread(1, core, (acrosses[0], right_part))
-    right_sums = [rotate(1, core, raw_rows, rows_here)]
+    rotate(1, core, raw_rows, rows_here)
     late.send_slot(core, 0, EARLY)
     go_raw(9, 5)
     gather_incoming()
@@ -519,7 +520,7 @@
     to_sibling_r.wait_recv()
     acrosses.append(across_of(rrecv, 1))
     spread(1, 1 - core, (acrosses[1], rrecv[1]))
-    right_sums.append(rotate(1, 1 - core, raw_rows, rows_here))
+    rotate(1, 1 - core, raw_rows, rows_here)
 
     late.send_slot(1 - core, 0, EARLY)
     late.send(EARLY, late_count)
@@ -537,7 +538,8 @@
     go_raw(raw_count, 9)
     go_late(1, 0)
     for entry, pair in enumerate((core, 1 - core)):
-        sums = right_sums[entry] + rotate(1, pair, 0, raw_rows)
+        late_part = rights[pair]
+        sums = jnp.sum(late_part * late_part, axis=0, keepdims=True) + rotate(1, pair, 0, raw_rows)
         esend[pair] = row_of(jnp.concatenate([left_sums[entry], sums], 1))
     e_sibling = remote(esend, epeer, refs.e_s.at[0], refs.e_r.at[0], sibling)
     e_sibling.start()
@@ -663,10 +665,23 @@
         copy.wait()
 
 
+def choose(ps_ref, branch_ref):
+    crossing = jnp.int32(0)
+    for pair in range(4):
+        crossing = crossing + jnp.where(ps_ref[pair] >= 4, 1, 0)
+    branch_ref[0] = jnp.maximum(crossing, 2) - 2
+
+
 def on_device(snapshots, partner_slot):
-    crossing = jnp.sum((partner_slot[:4] >= 4).astype(jnp.int32))
+    branch = pl.pallas_call(
+        choose,
+        out_shape=jax.ShapeDtypeStruct((1,), jnp.int32),
+        in_specs=[pl.BlockSpec(memory_space=pltpu.SMEM)],
+        out_specs=pl.BlockSpec(memory_space=pltpu.SMEM),
+        name="choose",
+    )(partner_slot)
     moved, energies = lax.switch(
-        jnp.maximum(crossing, 2) - 2,
+        branch[0],
         [functools.partial(call, cap) for cap in (2, 3, 4)],
         snapshots,
         partner_slot,

time: 64.9 us -> 64.8 us (level)
  other arithmetic: 1.29 us -> 0 us
  Pallas kernels: 61.7 us -> 62.9 us
    reduce_sum x1 -> x0, other arithmetic: 1.29 us -> none  [on_device(): crossing = jnp.sum((partner_slot[:4] >= 4).astype(jnp.int32))]
    pallas_call x0 -> x1, Pallas kernels: none -> 1.19 us  [on_device(): pl.pallas_call(choose, out_shape=jax.ShapeDtypeStruct((1,), jnp.int32), i...]
where the time goes in v6:
time: 64.8 us; the launch traced here: 64.6 us
  Pallas kernels  62.9 us (97%)
  between operations  1.47 us (2%)
    pallas_call x1, Pallas kernels, call(): pl.pallas_call(functools.partial(kernel, cap, tuple(scratch)), out_shape=...  60.4 us
    pallas_call x1, Pallas kernels, on_device(): pl.pallas_call(hand_out, out_shape=(jax.ShapeDtypeStruct(moved.shape, F32...  1.36 us

profile of v6, /device:TPU:1, one launch (start us, length us, event | category | flops | bytes accessed | tf_op | source)
XLA Modules:
  0.0 64.6 jit_solution(10908959763972335760)
XLA Ops:
  0.6 1.2 %choose.1 = s32[1]{0:T(128)} custom-call(s32[8]{0:T(128)} %ps_ref.1), custom_call_target="tpu_custom_call" | custom-call | tf_op jit(solution)/shard_map/choose/pallas_call | solution.py:676
  2.5 60.6 %conditional.1 = ((f32[512,1024]{1,0:T(8,128)S(1)}, f32[8,128]{1,0:T(8,128)S(1)})) conditional(s32[]{:T(128)} %bitcast, (f32[512,1024]{1,0:T(8,128)}, s32[8]{0:T(128)}) %tuple.17, (f32[512,1024]{1,0:T(8,128)}, s32[8]{0:T(128)}) %tuple.17, (f32[512,1024]{1,0:T(8,128)}, s32[8]{0:T(128)}) %tuple.17), branch_computations={%region_0.0_spmd, %region_1.0_spmd, %region_2.0_spmd} | conditional | bytes 8 | solution.py:683
  2.5 60.4 %round_2.1 = (f32[512,1024]{1,0:T(8,128)S(1)}, f32[8,128]{1,0:T(8,128)S(1)}) custom-call(f32[512,1024]{1,0:T(8,128)} %get-tuple-element.12.x_hbm, s32[8]{0:T(128)} %get-tuple-element.13.ps_any), custom_call_target="tpu_custom_call" | custom-call | tf_op jit(solution)/shard_map/cond/branch_0_fun/round_2/pallas_call | solution.py:640
  63.1 1.4 %hand_out.1 = (f32[512,1024]{1,0:T(8,128)}, f32[8,128]{1,0:T(8,128)}) custom-call(f32[512,1024]{1,0:T(8,128)S(1)} %get-tuple-element.24.moved_ref, f32[8,128]{1,0:T(8,128)S(1)} %get-tuple-element.25.energies_ref), custom_call_target="tpu_custom_call" | custom-call | tf_op jit(solution)/shard_map/hand_out/pallas_call | solution.py:690
